TPU v7x, 128 devices: a whole 4x4x4 slice. The times are simulated.
128 devices in a mesh: grp: 8 (over y, core), slc: 16 (over x, z).
Axes of the slice: x: 4, y: 4, z: 4, core: 2. Of those that a mesh axis runs over, the one named last changes fastest.
Arguments:
- tokens: bfloat16 [16384, 4096], P(('grp', 'slc')), may hold values from -6 to 6
- expert_ids: int32 [16384, 8], P(('grp', 'slc')), may hold values from 0 to 127, as said below
- slot_positions: int32 [16384, 8], P(('grp', 'slc')), may hold values from 0 to 10, as said below
- gate_probs: float32 [16384, 8], P(('grp', 'slc')), may hold values from 0.1 to 0.5
- w_gate: bfloat16 [128, 4096, 768], P(('grp', 'slc')), may hold values from -0.09375 to 0.09375
- w_up: bfloat16 [128, 4096, 768], P(('grp', 'slc')), may hold values from -0.09375 to 0.09375
- w_down: bfloat16 [128, 768, 4096], P(('grp', 'slc')), may hold values from -0.21875 to 0.21875
Outputs:
- moe_out: bfloat16 [16384, 4096], P(('grp', 'slc'))
Inputs may be any that keep to these rules, and one draw needn't show every extreme that they name: `expert_ids`: each token's 8 experts differ. Some expert is chosen by 10 or more tokens of every block of 128 tokens. `slot_positions`: within a block of 128 tokens, a choice's slot is the number of earlier choices of the block (tokens in order, then k in order) that name the same expert, or 10 where that number is 10 or more (the choice is dropped).
All inputs are finite; a program needn't handle non-finite values.
Results may differ from a plain program's by a relative error of at most 0.011.
Values may be sent and summed in bfloat16 or wider, within the bound.
A program may use at most 128 MiB of HBM per device.

v0:
```python
import jax
import jax.numpy as jnp
from jax import lax
from jax.sharding import PartitionSpec as P


def shards(tokens, expert_ids, slot_positions, gate_probs, w_gate, w_up, w_down):
    tok_rows, width = tokens.shape
    top_count = expert_ids.shape[1]
    experts = lax.axis_size(("grp", "slc")) * w_gate.shape[0]
    capacity = max(2, tok_rows * top_count * 5 // (4 * experts))
    kept = slot_positions < capacity
    dump = experts * capacity
    padded = jnp.concatenate([tokens, jnp.zeros((1, width), tokens.dtype)], 0)
    gate_w = w_gate[0]
    up_w = w_up[0]
    down_w = w_down[0]
    local_index = jnp.arange(tok_rows, dtype=jnp.int32)
    target = expert_ids * capacity + jnp.minimum(slot_positions, capacity - 1)
    target = jnp.where(kept, target, dump)
    sources = jnp.broadcast_to(local_index[:, None], target.shape).reshape(-1)
    table = jnp.full((dump + 1,), tok_rows, jnp.int32).at[target.reshape(-1)].set(sources)[:dump]
    outgoing = padded[table].reshape(experts, capacity, width)
    arrived = lax.all_to_all(outgoing, ("grp", "slc"), split_axis=0, concat_axis=0, tiled=True)
    flat_rows = arrived.reshape(-1, width)
    gate = jnp.dot(flat_rows, gate_w, preferred_element_type=jnp.float32)
    up = jnp.dot(flat_rows, up_w, preferred_element_type=jnp.float32)
    hidden = (jax.nn.silu(gate) * up).astype(jnp.bfloat16)
    result = jnp.dot(hidden, down_w, preferred_element_type=jnp.float32).astype(jnp.bfloat16)
    returned = lax.all_to_all(
        result.reshape(arrived.shape), ("grp", "slc"), split_axis=0, concat_axis=0, tiled=True
    )
    lookup = jnp.minimum(target, dump - 1)
    flat_out = returned.reshape(dump, width)
    picked = flat_out[lookup]
    weight = jnp.where(kept, gate_probs, jnp.float32(0.0))
    total = jnp.einsum("tk,tkd->td", weight, picked, preferred_element_type=jnp.float32)
    return total.astype(jnp.bfloat16)


def solution(mesh):
    in_specs = (
        P(("grp", "slc"), None),
        P(("grp", "slc"), None),
        P(("grp", "slc"), None),
        P(("grp", "slc"), None),
        P(("grp", "slc"), None, None),
        P(("grp", "slc"), None, None),
        P(("grp", "slc"), None, None),
    )
    out_specs = P(("grp", "slc"), None)
    return jax.shard_map(shards, mesh=mesh, in_specs=in_specs, out_specs=out_specs, check_vma=False)
```

profile of v0, /device:TPU:1, one launch (start us, length us, event | category | flops | bytes accessed | tf_op | source)
XLA Modules:
  0.0 581.8 jit_solution(13206250996200635141)
XLA Ops:
  0.0 0.7 compare_select_fusion.2
  0.7 0.1 copy.8
  0.8 0.1 reshape.46
  0.9 0.1 reshape.72
  1.0 4.3 scatter_custom_fusion
  5.4 1.3 concatenate.3
  6.7 8.3 %gather_fusion = bf16[1280,4096]{1,0:T(8,128)(2,1)} fusion(bf16[129,4096]{1,0:T(8,128)(2,1)S(1)} %concatenate.3, s32[2048]{0:T(1024)S(1)} %pad_clamp_fusion), kind=kCustom, calls=%fused_computation | custom fusion | bytes 20976640 | tf_op jit(solution)/shard_map/gather | solution.py:23
  15.0 15.6 %reshape.48 = bf16[128,10,4096]{2,1,0:T(8,128)(2,1)} reshape(bf16[1280,4096]{1,0:T(8,128)(2,1)} %gather_fusion) | data formatting | bytes 20971520 | tf_op jit(solution)/shard_map/reshape | solution.py:23
  30.6 200.7 %all_to_all.10 = bf16[128,10,4096]{2,1,0:T(8,128)(2,1)} all-to-all(bf16[128,10,4096]{2,1,0:T(8,128)(2,1)} %reshape.48), channel_id=1, replica_groups=mesh['grp'=8,'slc'=16] {'grp','slc'}, dimensions={0} | all-to-all | bytes 20971520 | tf_op jit(solution)/shard_map/all_to_all | solution.py:24
  231.3 16.5 %reshape.49 = bf16[1280,4096]{1,0:T(8,128)(2,1)} reshape(bf16[128,10,4096]{2,1,0:T(8,128)(2,1)} %all_to_all.10) | data formatting | bytes 20971520 | tf_op jit(solution)/shard_map/reshape | solution.py:25
  247.8 12.3 %fusion.5 = f32[1280,768]{1,0:T(8,128)S(1)} fusion(bf16[1280,4096]{1,0:T(8,128)(2,1)} %reshape.49, bf16[1,4096,768]{2,1,0:T(8,128)(2,1)} %param.11), kind=kOutput, calls=%fused_computation.9 | convolution fusion | flops 8053063680 | bytes 20709376 | tf_op jit(solution)/shard_map/dot_general | solution.py:26
  260.1 0.0 copy-done
  260.1 11.2 %fusion.10 = bf16[1280,768]{1,0:T(8,128)(2,1)S(1)} fusion(bf16[1280,4096]{1,0:T(8,128)(2,1)S(1)} %copy-done, bf16[1,4096,768]{2,1,0:T(8,128)(2,1)} %param.12, f32[1280,768]{1,0:T(8,128)S(1)} %fusion.5), kind=kOutput, calls=%fused_computation.12 | convolution fusion | flops 8058961920 | bytes 22675456 | tf_op jit(solution)/shard_map/dot_general | solution.py:27
  271.3 13.5 %convolution_convert_fusion = bf16[1280,4096]{1,0:T(8,128)(2,1)} fusion(bf16[1280,768]{1,0:T(8,128)(2,1)S(1)} %fusion.10, bf16[1,768,4096]{2,1,0:T(8,128)(2,1)} %param.13), kind=kOutput, calls=%fused_computation.3 | convolution fusion | flops 8058306560 | bytes 18743296 | tf_op jit(solution)/shard_map/dot_general | solution.py:29
  284.8 15.6 %reshape.50 = bf16[128,10,4096]{2,1,0:T(8,128)(2,1)} reshape(bf16[1280,4096]{1,0:T(8,128)(2,1)} %convolution_convert_fusion) | data formatting | bytes 20971520 | tf_op jit(solution)/shard_map/reshape | solution.py:31
  300.4 6.0 %all-to-all-start.1 = ((bf16[128,10,4096]{2,1,0:T(8,128)(2,1)}), bf16[128,10,4096]{2,1,0:T(8,128)(2,1)}, u32[]{:S(2)}, u32[]{:S(2)}) async-start(bf16[128,10,4096]{2,1,0:T(8,128)(2,1)} %reshape.50), calls=%async_computation.1 | async-start | bytes 33554432 | tf_op jit(solution)/shard_map/all_to_all | solution.py:30
  306.3 0.1 copy.9
  306.4 0.1 reshape.62
  306.6 0.1 copy.10
  306.7 230.4 %all-to-all-done.1 = bf16[128,10,4096]{2,1,0:T(8,128)(2,1)} async-done(((bf16[128,10,4096]{2,1,0:T(8,128)(2,1)}), bf16[128,10,4096]{2,1,0:T(8,128)(2,1)}, u32[]{:S(2)}, u32[]{:S(2)}) %all-to-all-start.1) | async-done | bytes 10485792 | tf_op jit(solution)/shard_map/all_to_all | solution.py:30
  537.1 16.5 %reshape.51 = bf16[1280,4096]{1,0:T(8,128)(2,1)} reshape(bf16[128,10,4096]{2,1,0:T(8,128)(2,1)} %all-to-all-done.1) | data formatting | bytes 20971520 | tf_op jit(solution)/shard_map/reshape | solution.py:34
  553.6 20.4 %gather_fusion.1 = bf16[1024,4096]{1,0:T(8,128)(2,1)} fusion(bf16[1280,4096]{1,0:T(8,128)(2,1)} %reshape.51, s32[1024]{0:T(1024)S(1)} %broadcast_clamp_fusion), kind=kCustom, calls=%fused_computation.1 | custom fusion | bytes 16781312 | tf_op jit(solution)/shard_map/gather | solution.py:35
  574.0 5.7 fusion
  579.7 2.1 copy.13
  (11 shorter events, 0.0 us)
Async XLA Ops:
  247.8 12.3 %copy-start = (bf16[1280,4096]{1,0:T(8,128)(2,1)S(1)}, bf16[1280,4096]{1,0:T(8,128)(2,1)}, u32[]{:S(2)}) copy-start(bf16[1280,4096]{1,0:T(8,128)(2,1)} %reshape.49) | copy-start | bytes 31457284
  300.4 6.2 %copy-start.1 = (s32[128,8]{0,1:T(8,128)S(1)}, s32[128,8]{0,1:T(8,128)}, u32[]{:S(2)}) copy-start(s32[128,8]{0,1:T(8,128)} %param.9) | copy-start | bytes 12292
  300.4 6.2 %copy-start.2 = (f32[128,8]{0,1:T(8,128)S(1)}, f32[128,8]{0,1:T(8,128)}, u32[]{:S(2)}) copy-start(f32[128,8]{0,1:T(8,128)} %param.10) | copy-start | bytes 12292
  300.4 236.7 %all-to-all-start.1 = ((bf16[128,10,4096]{2,1,0:T(8,128)(2,1)}), bf16[128,10,4096]{2,1,0:T(8,128)(2,1)}, u32[]{:S(2)}, u32[]{:S(2)}) async-start(bf16[128,10,4096]{2,1,0:T(8,128)(2,1)} %reshape.50), calls=%async_computation.1 | async-start | bytes 33554432 | tf_op jit(solution)/shard_map/all_to_all | solution.py:30
where the time goes:
time: 592 us; the launch traced here: 582 us
  waiting for transfers between devices  230 us (39%)
  blocking collectives  201 us (34%)
  local copies, waits for them, and re-layouts  101 us (17%)
  matrix products  42.7 us (7%)
  starting transfers between devices  5.95 us (1%)
    all_to_all x1, waiting for transfers between devices, shards(): lax.all_to_all(result.reshape(arrived.shape), ('grp', 'slc'), split_axis=...  230 us
    all_to_all x1, blocking collectives, shards(): lax.all_to_all(outgoing, ('grp', 'slc'), split_axis=0, concat_axis=0, til...  201 us
    gather x1, local copies, waits for them, and re-layouts, shards(): picked = flat_out[lookup]  20.4 us
    reshape x1, local copies, waits for them, and re-layouts, shards(): flat_out = returned.reshape(dump, width)  16.5 us
    reshape x1, local copies, waits for them, and re-layouts, shards(): flat_rows = arrived.reshape(-1, width)  16.5 us
    reshape x1, local copies, waits for them, and re-layouts, shards(): result.reshape(arrived.shape)  15.6 us
    reshape x1, local copies, waits for them, and re-layouts, shards(): outgoing = padded[table].reshape(experts, capacity, width)  15.6 us
    dot_general x1, matrix products, shards(): jnp.dot(hidden, down_w, preferred_element_type=jnp.float32)  13.5 us
  transfers between devices with their start and end apart: 1, of which 1 were waited for; matrix products, arithmetic and copies ran while one was open for 0% of the time, Pallas kernels for 0%

commit v1 on v0

v1 whole, which is shorter than its diff:
```python
import functools

import jax
import jax.numpy as jnp
import numpy as np
from jax import lax
from jax.experimental import pallas as pl
from jax.experimental.pallas import tpu as pltpu
from jax.sharding import PartitionSpec as P

MESH = pl.DeviceIdType.MESH
RING = 4
BLOCKS = 2 * RING
NT = 256
ORDERS = (("y", "x", "z"), ("x", "z", "y"), ("z", "y", "x"))


def chunk_widths(width):
    tiles = width // 128
    widths = [128 * ((tiles + 2 - r) // 3) for r in range(3)]
    return widths, [0, widths[0], widths[0] + widths[1]]


def swap_matrix(slots):
    unit = slots * BLOCKS
    q = np.arange(RING * unit)
    a, slot, c, b = q // unit, q % unit // BLOCKS, q % BLOCKS // RING, q % RING
    target = b * unit + slot * BLOCKS + c * RING + a
    return (np.arange(RING * unit)[:, None] == target[None, :]).astype(np.float32)


def column_tiles(width, body):
    full = width // NT

    @pl.loop(0, full)
    def _(n):
        body(pl.ds(pl.multiple_of(n * NT, NT), NT), NT)

    if width % NT:
        body(pl.ds(full * NT, width % NT), width % NT)


def kernel(slots, widths, starts, tok, meta, swap, wg, wu, wd, out,
           b2r0, b2r1, b2r2, b4r0, b4r1, b4r2, b5r0, b5r1, b5r2,
           g0, g1, g2, bs0, bs1, bs2, b30, b31, b32, sr0, sr1, sr2, rr0, rr1, rr2,
           km, kk, pp, sel, wc, comb, hid, hb, hc, wgv, wuv, wdv,
           wsem, own_sem, s1, r1, sm1, rm1, sf, rf, smf, rmf, s2, r2, s3, r3, l3,
           s4, r4, s5, r5, l5, ld5, s6, r6, s7, r7):
    b2r, b4r, b5r = (b2r0, b2r1, b2r2), (b4r0, b4r1, b4r2), (b5r0, b5r1, b5r2)
    g, bs, b3 = (g0, g1, g2), (bs0, bs1, bs2), (b30, b31, b32)
    sr, rr = (sr0, sr1, sr2), (rr0, rr1, rr2)
    unit = slots * BLOCKS
    rows = RING * unit
    toks = tok.shape[0]
    hidden = wdv.shape[0]
    grp, slc = lax.axis_index("grp"), lax.axis_index("slc")
    me = {"y": grp // 2, "c": lax.rem(grp, 2), "x": slc // RING, "z": lax.rem(slc, RING)}
    core = me["c"]
    mate = 1 - core

    def device(coords):
        return (coords["y"] * 2 + coords["c"], coords["x"] * RING + coords["z"])

    def at(**changes):
        return device({**me, **changes})

    def ahead(d, k):
        return lax.rem(me[d] + k, RING)

    def behind(d, k):
        return lax.rem(me[d] + RING - k, RING)

    def send(src, dst, ssem, rsem, where):
        return pltpu.make_async_remote_copy(
            src_ref=src, dst_ref=dst, send_sem=ssem, recv_sem=rsem, device_id=where, device_id_type=MESH
        )

    def local(src, dst, sem):
        return pltpu.make_async_copy(src, dst, sem)

    mate_id = at(c=mate)
    d1 = [o[0] for o in ORDERS]
    d2 = [o[1] for o in ORDERS]
    d3 = [o[2] for o in ORDERS]

    def w_in(n):
        cols = pl.ds(n * NT, NT)
        return (local(wg.at[:, cols], wgv.at[n % 2], wsem.at[2 * n]),
                local(wu.at[:, cols], wuv.at[n % 2], wsem.at[2 * n + 1]))

    h_tiles = hidden // NT
    for n in range(min(2, h_tiles)):
        for c in w_in(n):
            c.start()
    wd_in = local(wd, wdv, wsem.at[2 * h_tiles])
    wd_in.start()

    def tok_cols(r):
        return tok.at[:, pl.ds(starts[r], widths[r])]

    own_in = [local(tok_cols(r), g[r].at[core, me[d1[r]]], own_sem.at[r]) for r in range(3)]
    for c in own_in:
        c.start()

    barrier = pltpu.get_barrier_semaphore()
    greet = [mate_id] + [at(**{d: ahead(d, k)}) for d in ("x", "y", "z") for k in (1, 2, 3)]
    for where in greet:
        pl.semaphore_signal(barrier, inc=1, device_id=where, device_id_type=MESH)
    pl.semaphore_wait(barrier, len(greet))

    first, pending = [], []
    for r in range(3):
        mine = me[d1[r]]
        for i in range(3):
            where = at(**{d1[r]: ahead(d1[r], i + 1)})
            c = send(meta, km.at[r, core, mine], sm1.at[r, i], rm1.at[r, i], where)
            c.start()
            t = send(tok_cols(r), g[r].at[core, mine], s1.at[r, i], r1.at[r, i], where)
            t.start()
            first.append((r, i, c, t))
        c = send(meta, km.at[r, core, mine], smf.at[r, 0], rmf.at[r, 0], mate_id)
        c.start()
        t = send(tok_cols(r), g[r].at[core, mine], sf.at[r, 0], rf.at[r, 0], mate_id)
        t.start()
        pending += [c, t]
        km[r, core, mine] = meta[...]
    for i in range(3):
        for r in range(3):
            source = behind(d1[r], i + 1)
            _, _, c, t = first[3 * r + i]
            c.wait_recv()
            c2 = send(km.at[r, core, source], km.at[r, core, source], smf.at[r, i + 1], rmf.at[r, i + 1], mate_id)
            c2.start()
            t.wait_recv()
            t2 = send(g[r].at[core, source], g[r].at[core, source], sf.at[r, i + 1], rf.at[r, i + 1], mate_id)
            t2.start()
            pending += [c2, t2]
    for c in own_in:
        c.wait()
    for c in pending:
        c.wait_recv()
    for r in range(3):
        for k in range(8):
            kk[r, k] = jnp.concatenate([km[r, b // RING, b % RING, k : k + 1] for b in range(BLOCKS)], axis=0)
            pp[r, k] = jnp.concatenate([km[r, b // RING, b % RING, 8 + k : 9 + k] for b in range(BLOCKS)], axis=0)

    def route_key(r, p2, p3):
        place = {**me, d2[r]: p2, d3[r]: p3}
        expert = (place["y"] * 2 + core) * 16 + place["x"] * RING + place["z"]
        return expert * slots

    sub = lax.broadcasted_iota(jnp.int32, (BLOCKS, BLOCKS * toks), 0)
    lane = lax.broadcasted_iota(jnp.int32, (BLOCKS, BLOCKS * toks), 1)
    diagonal = (sub * toks <= lane) & (lane < sub * toks + toks)

    second = {}

    def dispatch(r, p2):
        @pl.loop(0, RING)
        def _(p3):
            base = route_key(r, p2, p3)
            keys = [kk[r, k] for k in range(8)]
            parts = []
            for slot in range(slots):
                key = (base + slot).astype(jnp.float32)
                hit = jnp.zeros((BLOCKS, toks), jnp.float32)
                for k in range(8):
                    hit = jnp.where(keys[k] == key, 1.0, hit)
                parts.append(jnp.where(diagonal, jnp.concatenate([hit] * BLOCKS, axis=1), 0.0))
            sel[pl.ds(pl.multiple_of(p3 * unit, unit), unit), :] = jnp.concatenate(parts, axis=0).astype(jnp.bfloat16)

        def tile(cols, size):
            data = g[r][:, :, :, cols].reshape(BLOCKS * toks, size)
            o = jnp.dot(sel[...], data, preferred_element_type=jnp.float32)
            bs[r][p2, :, :, cols] = o.astype(jnp.bfloat16).reshape(RING, unit, size)

        column_tiles(widths[r], tile)

    def second_send(r, i):
        p2 = ahead(d2[r], i + 1)
        return send(bs[r].at[p2], b2r[r].at[me[d2[r]]], s2.at[r, i], r2.at[r, i], at(**{d2[r]: p2}))

    @pl.loop(0, RING)
    def _(i):
        for r in range(3):
            dispatch(r, ahead(d2[r], i + 1))

            @pl.when(i < 3)
            def _():
                second_send(r, i).start()

    def third_source(r, i, p3):
        if i == 0:
            return bs[r].at[me[d2[r]], p3]
        return b2r[r].at[behind(d2[r], i), p3]

    def third_send(r, i, j):
        p3 = ahead(d3[r], j + 1)
        return send(third_source(r, i, p3), b3[r].at[me[d3[r]], behind(d2[r], i)],
                    s3.at[r, i, j], r3.at[r, i, j], at(**{d3[r]: p3}))

    def third_local(r, i):
        return local(third_source(r, i, me[d3[r]]), b3[r].at[me[d3[r]], behind(d2[r], i)], l3.at[r, i])

    for i in range(RING):
        for r in range(3):
            if i > 0:
                second_send(r, i - 1).wait_recv()
            for j in range(3):
                third_send(r, i, j).start()
            third_local(r, i).start()
    for i in range(RING):
        for r in range(3):
            third_local(r, i).wait()
            for j in range(3):
                third_send(r, i, j).wait_recv()

    def swap_rows(ref, index, width):
        def tile(cols, size):
            x = ref[(*index, slice(None), cols)].reshape(rows, size)
            y = jnp.dot(swap[...], x, preferred_element_type=jnp.float32)
            ref[(*index, slice(None), cols)] = y.astype(jnp.bfloat16).reshape(RING, unit, size)

        column_tiles(width, tile)

    @pl.loop(0, RING)
    def _(p):
        swap_rows(b3[1], (slice(None), p), widths[1])
        swap_rows(b3[2], (p, slice(None)), widths[2])

    for n in range(h_tiles):
        for c in w_in(n):
            c.wait()

        @pl.loop(0, RING)
        def _(p):
            gate = up = None
            for r in range(3):
                index = (p,) if r == 0 else (slice(None), p)
                x = b3[r][index].reshape(rows, widths[r])
                span = pl.ds(starts[r], widths[r])
                gr = jnp.dot(x, wgv[n % 2, span, :], preferred_element_type=jnp.float32)
                ur = jnp.dot(x, wuv[n % 2, span, :], preferred_element_type=jnp.float32)
                gate = gr if gate is None else gate + gr
                up = ur if up is None else up + ur
            h = gate / (1.0 + jnp.exp(-gate)) * up
            hid[p, :, :, n * NT : (n + 1) * NT] = h.astype(jnp.bfloat16).reshape(RING, unit, NT)

        if n + 2 < h_tiles:
            for c in w_in(n + 2):
                c.start()

    @pl.loop(0, RING)
    def _(p):
        x = hid[p].reshape(rows, hidden)
        y = jnp.dot(swap[...], x, preferred_element_type=jnp.float32)
        hb[:, p] = y.astype(jnp.bfloat16).reshape(RING, unit, hidden)
        x = hid[:, p].reshape(rows, hidden)
        y = jnp.dot(swap[...], x, preferred_element_type=jnp.float32)
        hc[p] = y.astype(jnp.bfloat16).reshape(RING, unit, hidden)

    wd_in.wait()
    for r in range(3):
        for i in range(3):
            second_send(r, i).wait_send()
            third_send(r, 0, i).wait_send()

    def fourth_send(r, i):
        p3 = ahead(d3[r], i + 1)
        return send(bs[r].at[p3], b4r[r].at[me[d3[r]]], s4.at[r, i], r4.at[r, i], at(**{d3[r]: p3}))

    @pl.loop(0, RING)
    def _(i):
        for r, h in enumerate((hid, hb, hc)):
            p3 = ahead(d3[r], i + 1)

            def tile(cols, size):
                x = h[p3].reshape(rows, hidden)
                w = wdv[:, pl.ds(pl.multiple_of(starts[r] + cols.start, 128), size)]
                o = jnp.dot(x, w, preferred_element_type=jnp.float32)
                bs[r][p3, :, :, cols] = o.astype(jnp.bfloat16).reshape(RING, unit, size)

            column_tiles(widths[r], tile)

            @pl.when(i < 3)
            def _():
                fourth_send(r, i).start()

    def fifth_source(r, i, p2):
        if i == 0:
            return bs[r].at[me[d3[r]], p2]
        return b4r[r].at[behind(d3[r], i), p2]

    def fifth_send(r, i, j):
        p2 = ahead(d2[r], j + 1)
        return send(fifth_source(r, i, p2), b5r[r].at[me[d2[r]], behind(d3[r], i)],
                    s5.at[r, i, j], r5.at[r, i, j], at(**{d2[r]: p2}))

    def fifth_local(r, i):
        return local(fifth_source(r, i, me[d2[r]]), b3[r].at[me[d2[r]], behind(d3[r], i)], l5.at[r, i])

    def fifth_load(r, i, j):
        e2, e3 = behind(d2[r], j + 1), behind(d3[r], i)
        return local(b5r[r].at[e2, e3], b3[r].at[e2, e3], ld5.at[r, i, j])

    for i in range(RING):
        for r in range(3):
            if i > 0:
                fourth_send(r, i - 1).wait_recv()
            for j in range(3):
                fifth_send(r, i, j).start()
            fifth_local(r, i).start()

    lanes = lax.broadcasted_iota(jnp.int32, (toks, RING * rows), 1)

    def sixth_send(r):
        return send(g[r].at[mate], sr[r], s6.at[r], r6.at[r], mate_id)

    for r in range(3):
        @pl.loop(0, RING * RING)
        def _(q):
            base = route_key(r, q // RING, lax.rem(q, RING))
            keys = [kk[r, k] for k in range(8)]
            probs = [pp[r, k] for k in range(8)]
            parts = []
            for slot in range(slots):
                key = (base + slot).astype(jnp.float32)
                weight = jnp.zeros((BLOCKS, toks), jnp.float32)
                for k in range(8):
                    weight = jnp.where(keys[k] == key, probs[k], weight)
                parts.append(weight)
            wc[pl.ds(pl.multiple_of(q * unit, unit), unit), :] = jnp.concatenate(parts, axis=0)

        turned = wc[...].T
        for b in range(BLOCKS):
            comb[b * toks : (b + 1) * toks, :] = jnp.where(lanes % BLOCKS == b, turned, 0.0).astype(jnp.bfloat16)

        for i in range(RING):
            for j in range(3):
                fifth_send(r, i, j).wait_recv()
                fifth_load(r, i, j).start()
        for c in pending[2 * r :: 6] + pending[2 * r + 1 :: 6]:
            c.wait_send()
        for i in range(RING):
            fifth_local(r, i).wait()
            for j in range(3):
                fifth_load(r, i, j).wait()

        def half(side):
            def tile(cols, size):
                x = b3[r][:, :, :, cols].reshape(RING * rows, size)
                w = comb[pl.ds(pl.multiple_of(side * RING * toks, RING * toks), RING * toks), :]
                o = jnp.dot(w, x, preferred_element_type=jnp.float32)
                g[r][side, :, :, cols] = o.astype(jnp.bfloat16).reshape(RING, toks, size)

            column_tiles(widths[r], tile)

        half(mate)
        sixth_send(r).start()
        half(core)

    def seventh_send(r, i):
        p1 = ahead(d1[r], i + 1)
        return send(g[r].at[core, p1], rr[r].at[i], s7.at[r, i], r7.at[r, i], at(**{d1[r]: p1}))

    for r in range(3):
        sixth_send(r).wait_recv()

        @pl.loop(0, RING)
        def _(i):
            p1 = ahead(d1[r], i + 1)
            total = g[r][core, p1].astype(jnp.float32) + sr[r][p1].astype(jnp.float32)
            g[r][core, p1] = total.astype(jnp.bfloat16)

            @pl.when(i < 3)
            def _():
                seventh_send(r, i).start()

    for r in range(3):
        total = g[r][core, me[d1[r]]].astype(jnp.float32)
        for i in range(3):
            seventh_send(r, i).wait_recv()
            total = total + rr[r][i].astype(jnp.float32)
        out[:, starts[r] : starts[r] + widths[r]] = total.astype(jnp.bfloat16)

    for _, _, c, t in first:
        c.wait_send()
        t.wait_send()
    for r in range(3):
        sixth_send(r).wait_send()
        for i in range(RING):
            for j in range(3):
                if i > 0:
                    third_send(r, i, j).wait_send()
                fifth_send(r, i, j).wait_send()
        for i in range(3):
            fourth_send(r, i).wait_send()
            seventh_send(r, i).wait_send()


def shards(tokens, expert_ids, slot_positions, gate_probs, w_gate, w_up, w_down):
    toks, width = tokens.shape
    experts = lax.axis_size(("grp", "slc"))
    slots = max(2, toks * expert_ids.shape[1] * 5 // (4 * experts))
    hidden = w_gate.shape[2]
    widths, starts = chunk_widths(width)
    unit = slots * BLOCKS
    keys = jnp.where(slot_positions < slots, expert_ids * slots + slot_positions, -1)
    meta = jnp.concatenate([keys.astype(jnp.float32).T, gate_probs.T], 0)
    swap = jnp.asarray(swap_matrix(slots), jnp.bfloat16)
    bf, f32 = jnp.bfloat16, jnp.float32
    hbm = [jax.ShapeDtypeStruct((RING, RING, unit, w), bf) for _ in range(3) for w in widths]
    dma = pltpu.SemaphoreType.DMA
    vmem = pltpu.VMEM
    scratch = (
        [vmem((2, RING, toks, w), bf) for w in widths]
        + [vmem((RING, RING, unit, w), bf) for w in widths]
        + [vmem((RING, RING, unit, w), bf) for w in widths]
        + [vmem((RING, toks, w), bf) for w in widths]
        + [vmem((3, toks, w), bf) for w in widths]
        + [
            vmem((3, 2, RING, 16, toks), f32),
            vmem((3, 8, BLOCKS, toks), f32),
            vmem((3, 8, BLOCKS, toks), f32),
            vmem((RING * unit, BLOCKS * toks), bf),
            vmem((RING * RING * unit, toks), f32),
            vmem((BLOCKS * toks, RING * RING * unit), bf),
            vmem((RING, RING, unit, hidden), bf),
            vmem((RING, RING, unit, hidden), bf),
            vmem((RING, RING, unit, hidden), bf),
            vmem((2, width, NT), bf),
            vmem((2, width, NT), bf),
            vmem((hidden, width), bf),
        ]
        + [dma((2 * (hidden // NT) + 1,)), dma((3,))]
        + [dma((3, 3))] * 4
        + [dma((3, 4))] * 4
        + [dma((3, 3))] * 2
        + [dma((3, 4, 3))] * 2
        + [dma((3, 4))]
        + [dma((3, 3))] * 2
        + [dma((3, 4, 3))] * 2
        + [dma((3, 4)), dma((3, 4, 3))]
        + [dma((3,))] * 2
        + [dma((3, 3))] * 2
    )
    any_spec = pl.BlockSpec(memory_space=pl.ANY)
    vmem_spec = pl.BlockSpec(memory_space=pltpu.VMEM)
    results = pl.pallas_call(
        functools.partial(kernel, slots, widths, starts),
        out_shape=[jax.ShapeDtypeStruct((toks, width), bf)] + hbm,
        in_specs=[any_spec, vmem_spec, vmem_spec, any_spec, any_spec, any_spec],
        out_specs=[vmem_spec] + [any_spec] * 9,
        scratch_shapes=scratch,
        compiler_params=pltpu.CompilerParams(
            collective_id=0, has_side_effects=True, vmem_limit_bytes=65000 * 1024
        ),
    )(tokens, meta, swap, w_gate.reshape(width, hidden), w_up.reshape(width, hidden), w_down.reshape(hidden, width))
    return results[0]


def solution(mesh):
    row = P(("grp", "slc"), None)
    cube = P(("grp", "slc"), None, None)
    return jax.shard_map(
        shards, mesh=mesh, in_specs=(row, row, row, row, cube, cube, cube), out_specs=row, check_vma=False
    )
```

time: 592 us -> 291 us (0.49); the launches traced: 582 us -> 291 us
  Pallas kernels: 0 us -> 286 us
  waiting for transfers between devices: 230 us -> 0 us
  blocking collectives: 201 us -> 0 us
  local copies, waits for them, and re-layouts: 101 us -> 2.29 us
  matrix products: 42.7 us -> 0 us
  starting transfers between devices: 5.95 us -> 0 us
    pallas_call x0 -> x1, Pallas kernels: none -> 286 us  [shards(): pl.pallas_call(functools.partial(kernel, slots, widths, starts), out_shap...]
    all_to_all x1 -> x0, waiting for transfers between devices: 230 us -> none  [shards(): lax.all_to_all(result.reshape(arrived.shape), ('grp', 'slc'), split_axis=...]
    all_to_all x1 -> x0, blocking collectives: 201 us -> none  [shards(): lax.all_to_all(outgoing, ('grp', 'slc'), split_axis=0, concat_axis=0, til...]
    reshape x6 -> x0, local copies, waits for them, and re-layouts: 64.4 us -> none  [the longest x1 16.5 us: shards(): flat_out = returned.reshape(dump, width)]
    dot_general x4 -> x0, matrix products: 42.7 us -> none  [the longest x1 13.5 us: shards(): jnp.dot(hidden, down_w, preferred_element_type=jnp.float32)]
    gather x2 -> x0, local copies, waits for them, and re-layouts: 28.7 us -> none  [the longest x1 20.4 us: shards(): picked = flat_out[lookup]]
    all_to_all x1 -> x0, starting transfers between devices: 5.95 us -> none  [shards(): lax.all_to_all(result.reshape(arrived.shape), ('grp', 'slc'), split_axis=...]
  transfers between devices with their start and end apart: 1 -> 0, of which waited for: 1 -> 0; matrix products, arithmetic and copies ran while one was open for 0% -> 0% of each run, Pallas kernels for 0% -> 0%
where the time goes in v1:
time: 291 us
  Pallas kernels  286 us (98%)
    pallas_call x1, Pallas kernels, shards(): pl.pallas_call(functools.partial(kernel, slots, widths, starts), out_shap...  286 us

profile of v1, /device:TPU:1, one launch (start us, length us, event | category | flops | bytes accessed | tf_op | source)
XLA Modules:
  0.0 290.8 jit_solution(6648601573361156719)
XLA Ops:
  0.0 0.7 convert_bitcast_fusion
  0.7 1.3 pad_maximum_fusion.meta
  2.0 286.5 %shard_map.82 = (bf16[128,4096]{1,0:T(8,128)(2,1)}, bf16[4,4,80,1408]{3,2,1,0:T(8,128)(2,1)}, bf16[4,4,80,1408]{3,2,1,0:T(8,128)(2,1)}, bf16[4,4,80,1280]{3,2,1,...) custom-call(bf16[128,4096]{1,0:T(8,128)(2,1)} %tok.1, ...), custom_call_target="tpu_custom_call" | custom-call | tf_op jit(solution)/shard_map/pallas_call | solution.py:449
  288.5 2.3 copy.10

commit v2 on v1

v2 whole, which is shorter than its diff:
```python
import functools

import jax
import jax.numpy as jnp
import numpy as np
from jax import lax
from jax.experimental import pallas as pl
from jax.experimental.pallas import tpu as pltpu
from jax.sharding import PartitionSpec as P

MESH = pl.DeviceIdType.MESH
RING = 4
BLOCKS = 2 * RING
NT = 256
ORDERS = (("y", "x", "z"), ("x", "z", "y"), ("z", "y", "x"))


def chunk_widths(width):
    tiles = width // 128
    widths = [128 * ((tiles + 2 - r) // 3) for r in range(3)]
    return widths, [0, widths[0], widths[0] + widths[1]]


def swap_matrix(slots):
    unit = slots * BLOCKS
    q = np.arange(RING * unit)
    a, slot, c, b = q // unit, q % unit // BLOCKS, q % BLOCKS // RING, q % RING
    target = b * unit + slot * BLOCKS + c * RING + a
    return (np.arange(RING * unit)[:, None] == target[None, :]).astype(np.float32)


def column_tiles(width):
    return [(n, min(NT, width - n)) for n in range(0, width, NT)]


def kernel(groups, widths, starts, tok, meta, swap0, swap1, wg, wu, wd, out, *refs):
    refs = list(refs)

    def take(count):
        taken, refs[:count] = refs[:count], []
        return taken

    b2r, b4r, b5r = ([take(3), take(3)] for _ in range(3))
    g = take(3)
    bs, b3 = ([take(3), take(3)] for _ in range(2))
    sr, rr = take(3), take(3)
    hid, hb, hc = (take(2) for _ in range(3))
    km, kk, pp, sel, wc, wgv, wuv, wdv = take(8)
    wsem, own_sem, s1, r1, sm1, rm1, sf, rf, smf, rmf = take(10)
    s2, r2, s3, r3, l3, s4, r4, s5, r5, l5, ld5, s6, r6, s7, r7 = take(15)
    swap = (swap0, swap1)
    units = [count * BLOCKS for _, count in groups]
    slots = sum(count for _, count in groups)
    toks = tok.shape[0]
    hidden = wdv.shape[0]
    grp, slc = lax.axis_index("grp"), lax.axis_index("slc")
    me = {"y": grp // 2, "c": lax.rem(grp, 2), "x": slc // RING, "z": lax.rem(slc, RING)}
    core = me["c"]
    mate = 1 - core

    def at(**changes):
        coords = {**me, **changes}
        return (coords["y"] * 2 + coords["c"], coords["x"] * RING + coords["z"])

    def ahead(d, k):
        return lax.rem(me[d] + k, RING)

    def behind(d, k):
        return lax.rem(me[d] + RING - k, RING)

    def send(src, dst, ssem, rsem, where):
        return pltpu.make_async_remote_copy(
            src_ref=src, dst_ref=dst, send_sem=ssem, recv_sem=rsem, device_id=where, device_id_type=MESH
        )

    def local(src, dst, sem):
        return pltpu.make_async_copy(src, dst, sem)

    mate_id = at(c=mate)
    d1 = [o[0] for o in ORDERS]
    d2 = [o[1] for o in ORDERS]
    d3 = [o[2] for o in ORDERS]
    h_tiles = hidden // NT
    uses = list(range(h_tiles)) + [(n + 1) % h_tiles for n in range(h_tiles)]
    places, loads = [], []
    held = {}
    for step, n in enumerate(uses):
        if n not in held:
            if len(held) < 2:
                place, after = len(held), -1
            else:
                oldest = uses[step - 2]
                place, after = held.pop(oldest), step - 2
            held[n] = place
            loads.append((step, n, place, after))
        places.append(held[n])

    def w_in(index):
        _, n, place, _ = loads[index]
        cols = pl.ds(n * NT, NT)
        return (local(wg.at[:, cols], wgv.at[place], wsem.at[2 * index]),
                local(wu.at[:, cols], wuv.at[place], wsem.at[2 * index + 1]))

    def loads_after(step):
        for index, (_, _, _, after) in enumerate(loads):
            if after == step:
                for c in w_in(index):
                    c.start()

    loads_after(-1)
    wd_in = local(wd, wdv, wsem.at[2 * len(loads)])
    wd_in.start()

    def tok_cols(r):
        return tok.at[:, pl.ds(starts[r], widths[r])]

    own_in = [local(tok_cols(r), g[r].at[core, me[d1[r]]], own_sem.at[r]) for r in range(3)]
    for c in own_in:
        c.start()

    barrier = pltpu.get_barrier_semaphore()
    greet = [mate_id] + [at(**{d: ahead(d, k)}) for d in ("x", "y", "z") for k in (1, 2, 3)]
    for where in greet:
        pl.semaphore_signal(barrier, inc=1, device_id=where, device_id_type=MESH)
    pl.semaphore_wait(barrier, len(greet))

    first, pending = [], []
    for r in range(3):
        mine = me[d1[r]]
        for i in range(3):
            where = at(**{d1[r]: ahead(d1[r], i + 1)})
            c = send(meta, km.at[r, core, mine], sm1.at[r, i], rm1.at[r, i], where)
            c.start()
            t = send(tok_cols(r), g[r].at[core, mine], s1.at[r, i], r1.at[r, i], where)
            t.start()
            first.append((c, t))
        c = send(meta, km.at[r, core, mine], smf.at[r, 0], rmf.at[r, 0], mate_id)
        c.start()
        t = send(tok_cols(r), g[r].at[core, mine], sf.at[r, 0], rf.at[r, 0], mate_id)
        t.start()
        pending += [c, t]
        km[r, core, mine] = meta[...]
    for i in range(3):
        for r in range(3):
            source = behind(d1[r], i + 1)
            c, t = first[3 * r + i]
            c.wait_recv()
            c2 = send(km.at[r, core, source], km.at[r, core, source], smf.at[r, i + 1], rmf.at[r, i + 1], mate_id)
            c2.start()
            t.wait_recv()
            t2 = send(g[r].at[core, source], g[r].at[core, source], sf.at[r, i + 1], rf.at[r, i + 1], mate_id)
            t2.start()
            pending += [c2, t2]
    for c in own_in:
        c.wait()
    for c in pending:
        c.wait_recv()
    for r in range(3):
        for k in range(8):
            kk[r, k] = jnp.concatenate([km[r, b // RING, b % RING, k : k + 1] for b in range(BLOCKS)], axis=0)
            pp[r, k] = jnp.concatenate([km[r, b // RING, b % RING, 8 + k : 9 + k] for b in range(BLOCKS)], axis=0)

    def route_key(r, p2, p3, slot):
        place = {**me, d2[r]: p2, d3[r]: p3}
        expert = (place["y"] * 2 + core) * 16 + place["x"] * RING + place["z"]
        return (expert * slots + slot).astype(jnp.float32)

    sub = lax.broadcasted_iota(jnp.int32, (BLOCKS, BLOCKS * toks), 0)
    lane = lax.broadcasted_iota(jnp.int32, (BLOCKS, BLOCKS * toks), 1)
    diagonal = (sub * toks <= lane) & (lane < sub * toks + toks)

    def second_send(a, r, i):
        p2 = ahead(d2[r], i + 1)
        return send(bs[a][r].at[p2], b2r[a][r].at[me[d2[r]]], s2.at[a, r, i], r2.at[a, r, i], at(**{d2[r]: p2}))

    def dispatch(a, r, pair):
        unit, (slot0, count) = units[a], groups[a]

        @pl.loop(0, 2 * RING)
        def _(q):
            p2 = jnp.where(q < RING, pair[0], pair[1])
            keys = [kk[r, k] for k in range(8)]
            parts = []
            for slot in range(count):
                key = route_key(r, p2, lax.rem(q, RING), slot0 + slot)
                hit = jnp.zeros((BLOCKS, toks), jnp.float32)
                for k in range(8):
                    hit = jnp.where(keys[k] == key, 1.0, hit)
                parts.append(jnp.where(diagonal, jnp.concatenate([hit] * BLOCKS, axis=1), 0.0))
            sel[pl.ds(pl.multiple_of(q * unit, unit), unit), :] = jnp.concatenate(parts, axis=0).astype(jnp.bfloat16)

        for n, size in column_tiles(widths[r]):
            data = g[r][:, :, :, n : n + size].reshape(BLOCKS * toks, size)
            o = jnp.dot(sel[: 2 * RING * unit], data, preferred_element_type=jnp.float32).astype(jnp.bfloat16)
            o = o.reshape(2, RING, unit, size)
            for e in range(2):
                bs[a][r][pair[e], :, :, n : n + size] = o[e]

    def dispatch_all(a, sending):
        @pl.loop(0, 2)
        def _(i):
            for r in range(3):
                dispatch(a, r, (ahead(d2[r], i + 1), ahead(d2[r], i + 3)))
                if sending:
                    @pl.when(i == 0)
                    def _():
                        second_send(a, r, 0).start()
                        second_send(a, r, 2).start()

                    @pl.when(i == 1)
                    def _():
                        second_send(a, r, 1).start()

    def third_source(a, r, i, p3):
        if i == 0:
            return bs[a][r].at[me[d2[r]], p3]
        return b2r[a][r].at[behind(d2[r], i), p3]

    def third_send(a, r, i, j):
        p3 = ahead(d3[r], j + 1)
        return send(third_source(a, r, i, p3), b3[a][r].at[me[d3[r]], behind(d2[r], i)],
                    s3.at[a, r, i, j], r3.at[a, r, i, j], at(**{d3[r]: p3}))

    def third_local(a, r, i):
        return local(third_source(a, r, i, me[d3[r]]), b3[a][r].at[me[d3[r]], behind(d2[r], i)], l3.at[a, r, i])

    def third_start(a, steps):
        for i in steps:
            for r in range(3):
                if i > 0:
                    second_send(a, r, i - 1).wait_recv()
                for j in range(3):
                    third_send(a, r, i, j).start()
                third_local(a, r, i).start()

    def third_finish(a):
        for i in range(RING):
            for r in range(3):
                third_local(a, r, i).wait()
                for j in range(3):
                    third_send(a, r, i, j).wait_recv()
        for r in range(3):
            for i in range(3):
                second_send(a, r, i).wait_send()
                third_send(a, r, 0, i).wait_send()

    def swap_rows(a):
        unit = units[a]

        @pl.loop(0, RING)
        def _(p):
            for n, size in column_tiles(widths[1]):
                x = b3[a][1][:, p, :, n : n + size].reshape(RING * unit, size)
                y = jnp.dot(swap[a][...], x, preferred_element_type=jnp.float32)
                bs[a][1][p, :, :, n : n + size] = y.astype(jnp.bfloat16).reshape(RING, unit, size)
            for n, size in column_tiles(widths[2]):
                x = b3[a][2][p, :, :, n : n + size].reshape(RING * unit, size)
                y = jnp.dot(swap[a][...], x, preferred_element_type=jnp.float32)
                bs[a][2][:, p, :, n : n + size] = y.astype(jnp.bfloat16).reshape(RING, unit, size)

    def up(a):
        unit = units[a]
        batch = 2
        for step in range(a * h_tiles, (a + 1) * h_tiles):
            n, place = uses[step], places[step]
            for index, (needed, _, _, _) in enumerate(loads):
                if needed == step:
                    for c in w_in(index):
                        c.wait()

            @pl.loop(0, RING // batch)
            def _(q):
                p = pl.ds(q * batch, batch)
                gate = lift = None
                for r, ref in enumerate((b3[a][0], bs[a][1], bs[a][2])):
                    x = ref[p].reshape(batch * RING * unit, widths[r])
                    span = pl.ds(starts[r], widths[r])
                    gr = jnp.dot(x, wgv[place, span, :], preferred_element_type=jnp.float32)
                    ur = jnp.dot(x, wuv[place, span, :], preferred_element_type=jnp.float32)
                    gate = gr if gate is None else gate + gr
                    lift = ur if lift is None else lift + ur
                h = gate / (1.0 + jnp.exp(-gate)) * lift
                hid[a][p, :, :, n * NT : (n + 1) * NT] = h.astype(jnp.bfloat16).reshape(batch, RING, unit, NT)

            loads_after(step)

    def swap_hidden(a):
        unit = units[a]

        @pl.loop(0, RING)
        def _(p):
            x = hid[a][p].reshape(RING * unit, hidden)
            y = jnp.dot(swap[a][...], x, preferred_element_type=jnp.float32)
            hb[a][:, p] = y.astype(jnp.bfloat16).reshape(RING, unit, hidden)
            x = hid[a][:, p].reshape(RING * unit, hidden)
            y = jnp.dot(swap[a][...], x, preferred_element_type=jnp.float32)
            hc[a][p] = y.astype(jnp.bfloat16).reshape(RING, unit, hidden)

    def fourth_send(a, r, i):
        p3 = ahead(d3[r], i + 1)
        return send(bs[a][r].at[p3], b4r[a][r].at[me[d3[r]]], s4.at[a, r, i], r4.at[a, r, i], at(**{d3[r]: p3}))

    def down(a):
        unit = units[a]

        @pl.loop(0, 2)
        def _(i):
            for r, h in enumerate((hid[a], hb[a], hc[a])):
                pair = (ahead(d3[r], i + 1), ahead(d3[r], i + 3))
                x = jnp.concatenate([h[p].reshape(RING * unit, hidden) for p in pair], axis=0)
                for n, size in column_tiles(widths[r]):
                    w = wdv[:, starts[r] + n : starts[r] + n + size]
                    o = jnp.dot(x, w, preferred_element_type=jnp.float32).astype(jnp.bfloat16)
                    o = o.reshape(2, RING, unit, size)
                    for e in range(2):
                        bs[a][r][pair[e], :, :, n : n + size] = o[e]

                @pl.when(i == 0)
                def _():
                    fourth_send(a, r, 0).start()
                    fourth_send(a, r, 2).start()

                @pl.when(i == 1)
                def _():
                    fourth_send(a, r, 1).start()

    def fifth_source(a, r, i, p2):
        if i == 0:
            return bs[a][r].at[me[d3[r]], p2]
        return b4r[a][r].at[behind(d3[r], i), p2]

    def fifth_send(a, r, i, j):
        p2 = ahead(d2[r], j + 1)
        return send(fifth_source(a, r, i, p2), b5r[a][r].at[me[d2[r]], behind(d3[r], i)],
                    s5.at[a, r, i, j], r5.at[a, r, i, j], at(**{d2[r]: p2}))

    def fifth_local(a, r, i):
        return local(fifth_source(a, r, i, me[d2[r]]), b3[a][r].at[me[d2[r]], behind(d3[r], i)], l5.at[a, r, i])

    def fifth_load(a, r, i, j):
        e2, e3 = behind(d2[r], j + 1), behind(d3[r], i)
        return local(b5r[a][r].at[e2, e3], b3[a][r].at[e2, e3], ld5.at[a, r, i, j])

    def fifth_start(a, steps):
        for i in steps:
            for r in range(3):
                if i > 0:
                    fourth_send(a, r, i - 1).wait_recv()
                for j in range(3):
                    fifth_send(a, r, i, j).start()
                fifth_local(a, r, i).start()

    def fifth_arrive(a, r):
        for i in range(RING):
            for j in range(3):
                fifth_send(a, r, i, j).wait_recv()
                fifth_load(a, r, i, j).start()

    def fifth_finish(a, r):
        for i in range(RING):
            fifth_local(a, r, i).wait()
            for j in range(3):
                fifth_load(a, r, i, j).wait()

    def weight_block(a, r, kb):
        if a == 0:
            return wgv.at[0, pl.ds(kb * BLOCKS * toks, BLOCKS * toks)]
        row = (2 * r + kb) * BLOCKS * toks
        return wuv.at[row // wuv.shape[1], pl.ds(row % wuv.shape[1], BLOCKS * toks)]

    def weigh(a, r):
        unit, (slot0, count) = units[a], groups[a]
        total = RING * RING * unit

        @pl.loop(0, RING * RING)
        def _(q):
            keys = [kk[r, k] for k in range(8)]
            probs = [pp[r, k] for k in range(8)]
            parts = []
            for slot in range(count):
                key = route_key(r, q // RING, lax.rem(q, RING), slot0 + slot)
                weight = jnp.zeros((BLOCKS, toks), jnp.float32)
                for k in range(8):
                    weight = jnp.where(keys[k] == key, probs[k], weight)
                parts.append(weight)
            wc[pl.ds(pl.multiple_of(q * unit, unit), unit), :] = jnp.concatenate(parts, axis=0)

        turned = wc[:total].T
        lanes = lax.broadcasted_iota(jnp.int32, (toks, NT), 1) % BLOCKS
        for kb in range(total // NT):
            part = turned[:, kb * NT : (kb + 1) * NT]
            target = weight_block(a, r, kb)
            for b in range(BLOCKS):
                target[b * toks : (b + 1) * toks, :] = jnp.where(lanes == b, part, 0.0).astype(jnp.bfloat16)

    def combine(a, r, side):
        rows = pl.ds(pl.multiple_of(side * RING * toks, RING * toks), RING * toks)
        blocks = RING * RING * units[a] // NT
        for n, size in column_tiles(widths[r]):
            x = b3[a][r][:, :, :, n : n + size].reshape(RING * RING * units[a], size)
            weights = jnp.concatenate([weight_block(a, r, kb)[rows, :] for kb in range(blocks)], axis=1)
            o = jnp.dot(weights, x, preferred_element_type=jnp.float32).reshape(RING, toks, size)
            if a:
                o = o + g[r][side, :, :, n : n + size].astype(jnp.float32)
            g[r][side, :, :, n : n + size] = o.astype(jnp.bfloat16)

    def sixth_send(r):
        return send(g[r].at[mate], sr[r], s6.at[r], r6.at[r], mate_id)

    def seventh_send(r, i):
        p1 = ahead(d1[r], i + 1)
        return send(g[r].at[core, p1], rr[r].at[i], s7.at[r, i], r7.at[r, i], at(**{d1[r]: p1}))

    dispatch_all(0, True)
    third_start(0, (0,))
    dispatch_all(1, False)
    third_start(0, (1, 2, 3))
    for r in range(3):
        for i in (0, 2, 1):
            second_send(1, r, i).start()
    third_start(1, (0,))
    third_finish(0)
    swap_rows(0)
    up(0)
    swap_hidden(0)
    wd_in.wait()
    third_start(1, (1, 2, 3))
    down(0)
    fifth_start(0, (0,))
    third_finish(1)
    swap_rows(1)
    up(1)
    swap_hidden(1)
    fifth_start(0, (1, 2, 3))
    down(1)
    fifth_start(1, (0,))
    for c in pending:
        c.wait_send()
    for r in range(3):
        weigh(1, r)
    for r in range(3):
        weigh(0, r)
        fifth_arrive(0, r)
        fifth_finish(0, r)
        combine(0, r, mate)
        combine(0, r, core)
    fifth_start(1, (1, 2, 3))
    for r in range(3):
        fifth_arrive(1, r)
        fifth_finish(1, r)
        combine(1, r, mate)
        sixth_send(r).start()
        combine(1, r, core)

    for r in range(3):
        sixth_send(r).wait_recv()

        @pl.loop(0, RING)
        def _(i):
            p1 = ahead(d1[r], i + 1)
            total = g[r][core, p1].astype(jnp.float32) + sr[r][p1].astype(jnp.float32)
            g[r][core, p1] = total.astype(jnp.bfloat16)

            @pl.when(i < 3)
            def _():
                seventh_send(r, i).start()

    for r in range(3):
        total = g[r][core, me[d1[r]]].astype(jnp.float32)
        for i in range(3):
            seventh_send(r, i).wait_recv()
            total = total + rr[r][i].astype(jnp.float32)
        out[:, starts[r] : starts[r] + widths[r]] = total.astype(jnp.bfloat16)

    for c, t in first:
        c.wait_send()
        t.wait_send()
    for r in range(3):
        sixth_send(r).wait_send()
        for i in range(3):
            seventh_send(r, i).wait_send()
        for a in range(2):
            for i in range(RING):
                for j in range(3):
                    if i > 0:
                        third_send(a, r, i, j).wait_send()
                    fifth_send(a, r, i, j).wait_send()
            for i in range(3):
                fourth_send(a, r, i).wait_send()


def shards(tokens, expert_ids, slot_positions, gate_probs, w_gate, w_up, w_down):
    toks, width = tokens.shape
    experts = lax.axis_size(("grp", "slc"))
    slots = max(2, toks * expert_ids.shape[1] * 5 // (4 * experts))
    lead = 2 * ((slots + 2) // 4)
    groups = ((0, lead), (lead, slots - lead))
    units = [count * BLOCKS for _, count in groups]
    hidden = w_gate.shape[2]
    widths, starts = chunk_widths(width)
    keys = jnp.where(slot_positions < slots, expert_ids * slots + slot_positions, -1)
    meta = jnp.concatenate([keys.astype(jnp.float32).T, gate_probs.T], 0)
    swaps = [jnp.asarray(swap_matrix(count), jnp.bfloat16) for _, count in groups]
    bf, f32 = jnp.bfloat16, jnp.float32
    hbm = [jax.ShapeDtypeStruct((RING, RING, u, w), bf) for _ in range(3) for u in units for w in widths]
    dma = pltpu.SemaphoreType.DMA
    vmem = pltpu.VMEM
    scratch = (
        [vmem((2, RING, toks, w), bf) for w in widths]
        + [vmem((RING, RING, u, w), bf) for _ in range(2) for u in units for w in widths]
        + [vmem((RING, toks, w), bf) for w in widths]
        + [vmem((3, toks, w), bf) for w in widths]
        + [vmem((RING, RING, u, hidden), bf) for _ in range(3) for u in units]
        + [
            vmem((3, 2, RING, 16, toks), f32),
            vmem((3, 8, BLOCKS, toks), f32),
            vmem((3, 8, BLOCKS, toks), f32),
            vmem((2 * RING * units[0], BLOCKS * toks), bf),
            vmem((RING * RING * units[0], toks), f32),
            vmem((2, width, NT), bf),
            vmem((2, width, NT), bf),
            vmem((hidden, width), bf),
        ]
        + [dma((16,)), dma((3,))]
        + [dma((3, 3))] * 4
        + [dma((3, 4))] * 4
        + [dma((2, 3, 3))] * 2
        + [dma((2, 3, 4, 3))] * 2
        + [dma((2, 3, 4))]
        + [dma((2, 3, 3))] * 2
        + [dma((2, 3, 4, 3))] * 2
        + [dma((2, 3, 4)), dma((2, 3, 4, 3))]
        + [dma((3,))] * 2
        + [dma((3, 3))] * 2
    )
    any_spec = pl.BlockSpec(memory_space=pl.ANY)
    vmem_spec = pl.BlockSpec(memory_space=pltpu.VMEM)
    results = pl.pallas_call(
        functools.partial(kernel, groups, widths, starts),
        out_shape=[jax.ShapeDtypeStruct((toks, width), bf)] + hbm,
        in_specs=[any_spec, vmem_spec, vmem_spec, vmem_spec, any_spec, any_spec, any_spec],
        out_specs=[vmem_spec] + [any_spec] * len(hbm),
        scratch_shapes=scratch,
        compiler_params=pltpu.CompilerParams(
            collective_id=0, has_side_effects=True, vmem_limit_bytes=65000 * 1024
        ),
    )(tokens, meta, *swaps, w_gate.reshape(width, hidden), w_up.reshape(width, hidden), w_down.reshape(hidden, width))
    return results[0]


def solution(mesh):
    row = P(("grp", "slc"), None)
    cube = P(("grp", "slc"), None, None)
    return jax.shard_map(
        shards, mesh=mesh, in_specs=(row, row, row, row, cube, cube, cube), out_specs=row, check_vma=False
    )
```

time: 291 us -> 228 us (0.78)
  Pallas kernels: 286 us -> 223 us
    pallas_call x1, Pallas kernels: 286 us -> 223 us  [shards(): pl.pallas_call(functools.partial(kernel, groups, widths, starts), out_sha...]
where the time goes in v2:
time: 228 us; the launch traced here: 227 us
  Pallas kernels  223 us (98%)
  local copies, waits for them, and re-layouts  2.29 us (1%)
    pallas_call x1, Pallas kernels, shards(): pl.pallas_call(functools.partial(kernel, groups, widths, starts), out_sha...  223 us

profile of v2, /device:TPU:1, one launch (start us, length us, event | category | flops | bytes accessed | tf_op | source)
XLA Modules:
  0.0 227.1 jit_solution(1102110240117714732)
XLA Ops:
  0.0 0.7 convert_bitcast_fusion
  0.7 1.3 pad_maximum_fusion.meta
  2.0 222.8 %shard_map.91 = (bf16[128,4096]{1,0:T(8,128)(2,1)}, bf16[4,4,48,1408]{3,2,1,0:T(8,128)(2,1)}, bf16[4,4,48,1408]{3,2,1,0:T(8,128)(2,1)}, bf16[4,4,48,1280]{3,2,1,...) custom-call(bf16[128,4096]{1,0:T(8,128)(2,1)} %tok.1, ...), custom_call_target="tpu_custom_call" | custom-call | tf_op jit(solution)/shard_map/pallas_call | solution.py:538
  224.8 2.3 %copy.11 = bf16[128,4096]{1,0:T(8,128)(2,1)} copy(bf16[128,4096]{1,0:T(8,128)(2,1)} %get-tuple-element.6) | data formatting | bytes 2097152

commit v3 on v2

--- a/solution.py
+++ b/solution.py
@@ -33,7 +33,7 @@
     return [(n, min(NT, width - n)) for n in range(0, width, NT)]
 
 
-def kernel(groups, widths, starts, tok, meta, swap0, swap1, wg, wu, wd, out, *refs):
+def kernel(groups, widths, starts, tok, ids, places_in, probs_in, swap0, swap1, wg, wu, wd, out, *refs):
     refs = list(refs)
 
     def take(count):
@@ -45,8 +45,8 @@
     bs, b3 = ([take(3), take(3)] for _ in range(2))
     sr, rr = take(3), take(3)
     hid, hb, hc = (take(2) for _ in range(3))
-    km, kk, pp, sel, wc, wgv, wuv, wdv = take(8)
-    wsem, own_sem, s1, r1, sm1, rm1, sf, rf, smf, rmf = take(10)
+    meta, km, kk, pp, sel, wc, wgv, wuv, wdv = take(9)
+    wsem, own_sem, s1, r1, sb, rb, sm1, rm1, sf, rf, smf, rmf = take(12)
     s2, r2, s3, r3, l3, s4, r4, s5, r5, l5, ld5, s6, r6, s7, r7 = take(15)
     swap = (swap0, swap1)
     units = [count * BLOCKS for _, count in groups]
@@ -107,6 +107,9 @@
                 for c in w_in(index):
                     c.start()
 
+    chosen = jnp.where(places_in[...] < slots, ids[...] * slots + places_in[...], -1)
+    meta[0:8] = chosen.astype(jnp.float32)
+    meta[8:16] = probs_in[...]
     loads_after(-1)
     wd_in = local(wd, wdv, wsem.at[2 * len(loads)])
     wd_in.start()
@@ -124,36 +127,67 @@
         pl.semaphore_signal(barrier, inc=1, device_id=where, device_id_type=MESH)
     pl.semaphore_wait(barrier, len(greet))
 
-    first, pending = [], []
+    half = toks // 2
+    lower, upper = pl.ds(0, half), pl.ds(half, half)
+    ways = ((1, (lower, upper)), (3, (upper, lower)))
+    first, pending, relays = [], [], []
+
+    def to_mate(r, source, rows, index):
+        ref = g[r].at[core, source, rows]
+        c = send(ref, ref, sf.at[r, index], rf.at[r, index], mate_id)
+        c.start()
+        pending.append((r, c))
+
+    routes = []
     for r in range(3):
         mine = me[d1[r]]
         for i in range(3):
-            where = at(**{d1[r]: ahead(d1[r], i + 1)})
-            c = send(meta, km.at[r, core, mine], sm1.at[r, i], rm1.at[r, i], where)
+            c = send(meta, km.at[r, core, mine], sm1.at[r, i], rm1.at[r, i], at(**{d1[r]: ahead(d1[r], i + 1)}))
             c.start()
-            t = send(tok_cols(r), g[r].at[core, mine], s1.at[r, i], r1.at[r, i], where)
-            t.start()
-            first.append((c, t))
+            routes.append((r, i, c))
         c = send(meta, km.at[r, core, mine], smf.at[r, 0], rmf.at[r, 0], mate_id)
         c.start()
-        t = send(tok_cols(r), g[r].at[core, mine], sf.at[r, 0], rf.at[r, 0], mate_id)
-        t.start()
-        pending += [c, t]
+        pending.append((r, c))
+    near = {}
+    for h in range(2):
+        for r in range(3):
+            mine = me[d1[r]]
+            for w, (way, halves) in enumerate(ways):
+                src = tok.at[halves[h], pl.ds(starts[r], widths[r])]
+                c = send(src, g[r].at[core, mine, halves[h]], s1.at[r, w, h], r1.at[r, w, h], at(**{d1[r]: ahead(d1[r], way)}))
+                c.start()
+                near[r, w, h] = c
+    for r in range(3):
+        mine = me[d1[r]]
+        c = send(tok_cols(r), g[r].at[core, mine], sf.at[r, 0], rf.at[r, 0], mate_id)
+        c.start()
+        pending.append((r, c))
         km[r, core, mine] = meta[...]
-    for i in range(3):
-        for r in range(3):
-            source = behind(d1[r], i + 1)
-            c, t = first[3 * r + i]
-            c.wait_recv()
-            c2 = send(km.at[r, core, source], km.at[r, core, source], smf.at[r, i + 1], rmf.at[r, i + 1], mate_id)
-            c2.start()
-            t.wait_recv()
-            t2 = send(g[r].at[core, source], g[r].at[core, source], sf.at[r, i + 1], rf.at[r, i + 1], mate_id)
-            t2.start()
-            pending += [c2, t2]
+    for h in range(2):
+        for r in range(3):
+            for w, (way, halves) in enumerate(ways):
+                source = behind(d1[r], way)
+                near[r, w, h].wait_recv()
+                if h == 0:
+                    ref = g[r].at[core, source, halves[0]]
+                    c = send(ref, ref, sb.at[r, w], rb.at[r, w], at(**{d1[r]: ahead(d1[r], way)}))
+                    c.start()
+                    relays.append((r, w, c))
+                to_mate(r, source, halves[h], 1 + 2 * w + h)
+        if h == 0:
+            for r, i, c in routes:
+                source = behind(d1[r], i + 1)
+                c.wait_recv()
+                c = send(km.at[r, core, source], km.at[r, core, source], smf.at[r, i + 1], rmf.at[r, i + 1], mate_id)
+                c.start()
+                pending.append((r, c))
+    for r, w, c in relays:
+        c.wait_recv()
+        to_mate(r, behind(d1[r], 2), ways[w][1][0], 5 + w)
+    first = [c for _, _, c in routes] + list(near.values())
     for c in own_in:
         c.wait()
-    for c in pending:
+    for _, c in pending:
         c.wait_recv()
     for r in range(3):
         for k in range(8):
@@ -296,11 +330,28 @@
             y = jnp.dot(swap[a][...], x, preferred_element_type=jnp.float32)
             hc[a][p] = y.astype(jnp.bfloat16).reshape(RING, unit, hidden)
 
-    def fourth_send(a, r, i):
+    def part_tiles(r, part):
+        tiles = column_tiles(widths[r])
+        middle = (len(tiles) + 1) // 2
+        return tiles[:middle] if part == 0 else tiles[middle:]
+
+    def part_cols(r, part):
+        tiles = part_tiles(r, part)
+        return tiles[0][0], tiles[-1][0] + tiles[-1][1] - tiles[0][0]
+
+    def back_tiles(a, r, part):
+        return part_tiles(r, part) if a else column_tiles(widths[r])
+
+    def back_cols(a, r, part):
+        return pl.ds(*part_cols(r, part)) if a else pl.ds(0, widths[r])
+
+    def fourth_send(a, part, r, i):
         p3 = ahead(d3[r], i + 1)
-        return send(bs[a][r].at[p3], b4r[a][r].at[me[d3[r]]], s4.at[a, r, i], r4.at[a, r, i], at(**{d3[r]: p3}))
-
-    def down(a):
+        cols = back_cols(a, r, part)
+        return send(bs[a][r].at[p3, :, :, cols], b4r[a][r].at[me[d3[r]], :, :, cols],
+                    s4.at[a + part, r, i], r4.at[a + part, r, i], at(**{d3[r]: p3}))
+
+    def down(a, part):
         unit = units[a]
 
         @pl.loop(0, 2)
@@ -308,7 +359,7 @@
             for r, h in enumerate((hid[a], hb[a], hc[a])):
                 pair = (ahead(d3[r], i + 1), ahead(d3[r], i + 3))
                 x = jnp.concatenate([h[p].reshape(RING * unit, hidden) for p in pair], axis=0)
-                for n, size in column_tiles(widths[r]):
+                for n, size in back_tiles(a, r, part):
                     w = wdv[:, starts[r] + n : starts[r] + n + size]
                     o = jnp.dot(x, w, preferred_element_type=jnp.float32).astype(jnp.bfloat16)
                     o = o.reshape(2, RING, unit, size)
@@ -317,50 +368,53 @@
 
                 @pl.when(i == 0)
                 def _():
-                    fourth_send(a, r, 0).start()
-                    fourth_send(a, r, 2).start()
+                    fourth_send(a, part, r, 0).start()
+                    fourth_send(a, part, r, 2).start()
 
                 @pl.when(i == 1)
                 def _():
-                    fourth_send(a, r, 1).start()
-
-    def fifth_source(a, r, i, p2):
+                    fourth_send(a, part, r, 1).start()
+
+    def fifth_source(a, part, r, i, p2):
+        cols = back_cols(a, r, part)
         if i == 0:
-            return bs[a][r].at[me[d3[r]], p2]
-        return b4r[a][r].at[behind(d3[r], i), p2]
-
-    def fifth_send(a, r, i, j):
+            return bs[a][r].at[me[d3[r]], p2, :, cols]
+        return b4r[a][r].at[behind(d3[r], i), p2, :, cols]
+
+    def fifth_send(a, part, r, i, j):
         p2 = ahead(d2[r], j + 1)
-        return send(fifth_source(a, r, i, p2), b5r[a][r].at[me[d2[r]], behind(d3[r], i)],
-                    s5.at[a, r, i, j], r5.at[a, r, i, j], at(**{d2[r]: p2}))
-
-    def fifth_local(a, r, i):
-        return local(fifth_source(a, r, i, me[d2[r]]), b3[a][r].at[me[d2[r]], behind(d3[r], i)], l5.at[a, r, i])
-
-    def fifth_load(a, r, i, j):
-        e2, e3 = behind(d2[r], j + 1), behind(d3[r], i)
-        return local(b5r[a][r].at[e2, e3], b3[a][r].at[e2, e3], ld5.at[a, r, i, j])
-
-    def fifth_start(a, steps):
+        return send(fifth_source(a, part, r, i, p2), b5r[a][r].at[me[d2[r]], behind(d3[r], i), :, back_cols(a, r, part)],
+                    s5.at[a + part, r, i, j], r5.at[a + part, r, i, j], at(**{d2[r]: p2}))
+
+    def fifth_local(a, part, r, i):
+        mine = me[d2[r]]
+        return local(fifth_source(a, part, r, i, mine), b3[a][r].at[mine, behind(d3[r], i), :, back_cols(a, r, part)],
+                     l5.at[a + part, r, i])
+
+    def fifth_load(a, part, r, i, j):
+        e2, e3, cols = behind(d2[r], j + 1), behind(d3[r], i), back_cols(a, r, part)
+        return local(b5r[a][r].at[e2, e3, :, cols], b3[a][r].at[e2, e3, :, cols], ld5.at[a + part, r, i, j])
+
+    def fifth_start(a, part, steps):
         for i in steps:
             for r in range(3):
                 if i > 0:
-                    fourth_send(a, r, i - 1).wait_recv()
+                    fourth_send(a, part, r, i - 1).wait_recv()
                 for j in range(3):
-                    fifth_send(a, r, i, j).start()
-                fifth_local(a, r, i).start()
-
-    def fifth_arrive(a, r):
+                    fifth_send(a, part, r, i, j).start()
+                fifth_local(a, part, r, i).start()
+
+    def fifth_arrive(a, part, r):
         for i in range(RING):
             for j in range(3):
-                fifth_send(a, r, i, j).wait_recv()
-                fifth_load(a, r, i, j).start()
-
-    def fifth_finish(a, r):
+                fifth_send(a, part, r, i, j).wait_recv()
+                fifth_load(a, part, r, i, j).start()
+
+    def fifth_finish(a, part, r):
         for i in range(RING):
-            fifth_local(a, r, i).wait()
+            fifth_local(a, part, r, i).wait()
             for j in range(3):
-                fifth_load(a, r, i, j).wait()
+                fifth_load(a, part, r, i, j).wait()
 
     def weight_block(a, r, kb):
         if a == 0:
@@ -393,10 +447,10 @@
             for b in range(BLOCKS):
                 target[b * toks : (b + 1) * toks, :] = jnp.where(lanes == b, part, 0.0).astype(jnp.bfloat16)
 
-    def combine(a, r, side):
+    def combine(a, r, side, tiles):
         rows = pl.ds(pl.multiple_of(side * RING * toks, RING * toks), RING * toks)
         blocks = RING * RING * units[a] // NT
-        for n, size in column_tiles(widths[r]):
+        for n, size in tiles:
             x = b3[a][r][:, :, :, n : n + size].reshape(RING * RING * units[a], size)
             weights = jnp.concatenate([weight_block(a, r, kb)[rows, :] for kb in range(blocks)], axis=1)
             o = jnp.dot(weights, x, preferred_element_type=jnp.float32).reshape(RING, toks, size)
@@ -404,12 +458,15 @@
                 o = o + g[r][side, :, :, n : n + size].astype(jnp.float32)
             g[r][side, :, :, n : n + size] = o.astype(jnp.bfloat16)
 
-    def sixth_send(r):
-        return send(g[r].at[mate], sr[r], s6.at[r], r6.at[r], mate_id)
-
-    def seventh_send(r, i):
+    def sixth_send(r, part):
+        cols = pl.ds(*part_cols(r, part))
+        return send(g[r].at[mate, :, :, cols], sr[r].at[:, :, cols], s6.at[r, part], r6.at[r, part], mate_id)
+
+    def seventh_send(r, part, i):
         p1 = ahead(d1[r], i + 1)
-        return send(g[r].at[core, p1], rr[r].at[i], s7.at[r, i], r7.at[r, i], at(**{d1[r]: p1}))
+        n, size = part_cols(r, part)
+        return send(g[r].at[core, p1, :, pl.ds(n, size)], rr[r].at[i, :, pl.ds(n, size)],
+                    s7.at[r, part, i], r7.at[r, part, i], at(**{d1[r]: p1}))
 
     dispatch_all(0, True)
     third_start(0, (0,))
@@ -425,68 +482,76 @@
     swap_hidden(0)
     wd_in.wait()
     third_start(1, (1, 2, 3))
-    down(0)
-    fifth_start(0, (0,))
+    down(0, 0)
+    fifth_start(0, 0, (0,))
     third_finish(1)
     swap_rows(1)
     up(1)
     swap_hidden(1)
-    fifth_start(0, (1, 2, 3))
-    down(1)
-    fifth_start(1, (0,))
-    for c in pending:
+    fifth_start(0, 0, (1, 2, 3))
+    for part in range(2):
+        down(1, part)
+        fifth_start(1, part, (0,))
+    for c in [c for _, c in pending] + [c for _, _, c in relays]:
         c.wait_send()
     for r in range(3):
         weigh(1, r)
     for r in range(3):
         weigh(0, r)
-        fifth_arrive(0, r)
-        fifth_finish(0, r)
-        combine(0, r, mate)
-        combine(0, r, core)
-    fifth_start(1, (1, 2, 3))
-    for r in range(3):
-        fifth_arrive(1, r)
-        fifth_finish(1, r)
-        combine(1, r, mate)
-        sixth_send(r).start()
-        combine(1, r, core)
-
-    for r in range(3):
-        sixth_send(r).wait_recv()
-
-        @pl.loop(0, RING)
-        def _(i):
-            p1 = ahead(d1[r], i + 1)
-            total = g[r][core, p1].astype(jnp.float32) + sr[r][p1].astype(jnp.float32)
-            g[r][core, p1] = total.astype(jnp.bfloat16)
-
-            @pl.when(i < 3)
-            def _():
-                seventh_send(r, i).start()
-
-    for r in range(3):
-        total = g[r][core, me[d1[r]]].astype(jnp.float32)
-        for i in range(3):
-            seventh_send(r, i).wait_recv()
-            total = total + rr[r][i].astype(jnp.float32)
-        out[:, starts[r] : starts[r] + widths[r]] = total.astype(jnp.bfloat16)
-
-    for c, t in first:
+        fifth_arrive(0, 0, r)
+        fifth_finish(0, 0, r)
+        combine(0, r, mate, column_tiles(widths[r]))
+        combine(0, r, core, column_tiles(widths[r]))
+    for part in range(2):
+        fifth_start(1, part, (1, 2, 3))
+
+    for part in range(2):
+        for r in range(3):
+            fifth_arrive(1, part, r)
+        for r in range(3):
+            fifth_finish(1, part, r)
+            combine(1, r, mate, part_tiles(r, part))
+            sixth_send(r, part).start()
+        for r in range(3):
+            combine(1, r, core, part_tiles(r, part))
+        for r in range(3):
+            sixth_send(r, part).wait_recv()
+            n, size = part_cols(r, part)
+
+            for i in range(3):
+                p1 = ahead(d1[r], i + 1)
+                total = g[r][core, p1, :, n : n + size].astype(jnp.float32) + sr[r][p1, :, n : n + size].astype(jnp.float32)
+                g[r][core, p1, :, n : n + size] = total.astype(jnp.bfloat16)
+                seventh_send(r, part, i).start()
+
+    for part in range(2):
+        for r in range(3):
+            n, size = part_cols(r, part)
+            mine = me[d1[r]]
+            total = g[r][core, mine, :, n : n + size].astype(jnp.float32) + sr[r][mine, :, n : n + size].astype(jnp.float32)
+            for i in range(3):
+                seventh_send(r, part, i).wait_recv()
+                total = total + rr[r][i, :, n : n + size].astype(jnp.float32)
+            out[:, starts[r] + n : starts[r] + n + size] = total.astype(jnp.bfloat16)
+
+    for r in range(3):
+        for part in range(2):
+            sixth_send(r, part).wait_send()
+            for i in range(3):
+                seventh_send(r, part, i).wait_send()
+    for c in first:
         c.wait_send()
-        t.wait_send()
-    for r in range(3):
-        sixth_send(r).wait_send()
-        for i in range(3):
-            seventh_send(r, i).wait_send()
+    for r in range(3):
         for a in range(2):
             for i in range(RING):
                 for j in range(3):
                     if i > 0:
                         third_send(a, r, i, j).wait_send()
-                    fifth_send(a, r, i, j).wait_send()
+                    for part in range(1 + a):
+                        fifth_send(a, part, r, i, j).wait_send()
             for i in range(3):
-                fourth_send(a, r, i).wait_send()
+                for part in range(1 + a):
+                    fourth_send(a, part, r, i).wait_send()
 
 
 def shards(tokens, expert_ids, slot_positions, gate_probs, w_gate, w_up, w_down):
@@ -498,8 +563,6 @@
     units = [count * BLOCKS for _, count in groups]
     hidden = w_gate.shape[2]
     widths, starts = chunk_widths(width)
-    keys = jnp.where(slot_positions < slots, expert_ids * slots + slot_positions, -1)
-    meta = jnp.concatenate([keys.astype(jnp.float32).T, gate_probs.T], 0)
     swaps = [jnp.asarray(swap_matrix(count), jnp.bfloat16) for _, count in groups]
     bf, f32 = jnp.bfloat16, jnp.float32
     hbm = [jax.ShapeDtypeStruct((RING, RING, u, w), bf) for _ in range(3) for u in units for w in widths]
@@ -512,6 +575,7 @@
         + [vmem((3, toks, w), bf) for w in widths]
         + [vmem((RING, RING, u, hidden), bf) for _ in range(3) for u in units]
         + [
+            vmem((16, toks), f32),
             vmem((3, 2, RING, 16, toks), f32),
             vmem((3, 8, BLOCKS, toks), f32),
             vmem((3, 8, BLOCKS, toks), f32),
@@ -522,29 +586,33 @@
             vmem((hidden, width), bf),
         ]
         + [dma((16,)), dma((3,))]
-        + [dma((3, 3))] * 4
-        + [dma((3, 4))] * 4
+        + [dma((3, 2, 2))] * 2
+        + [dma((3, 2))] * 2
+        + [dma((3, 3))] * 2
+        + [dma((3, 7))] * 2
+        + [dma((3, 4))] * 2
         + [dma((2, 3, 3))] * 2
         + [dma((2, 3, 4, 3))] * 2
         + [dma((2, 3, 4))]
-        + [dma((2, 3, 3))] * 2
-        + [dma((2, 3, 4, 3))] * 2
-        + [dma((2, 3, 4)), dma((2, 3, 4, 3))]
-        + [dma((3,))] * 2
-        + [dma((3, 3))] * 2
+        + [dma((3, 3, 3))] * 2
+        + [dma((3, 3, 4, 3))] * 2
+        + [dma((3, 3, 4)), dma((3, 3, 4, 3))]
+        + [dma((3, 2))] * 2
+        + [dma((3, 2, 3))] * 2
     )
     any_spec = pl.BlockSpec(memory_space=pl.ANY)
     vmem_spec = pl.BlockSpec(memory_space=pltpu.VMEM)
     results = pl.pallas_call(
         functools.partial(kernel, groups, widths, starts),
         out_shape=[jax.ShapeDtypeStruct((toks, width), bf)] + hbm,
-        in_specs=[any_spec, vmem_spec, vmem_spec, vmem_spec, any_spec, any_spec, any_spec],
+        in_specs=[any_spec] + [vmem_spec] * 5 + [any_spec] * 3,
         out_specs=[vmem_spec] + [any_spec] * len(hbm),
         scratch_shapes=scratch,
         compiler_params=pltpu.CompilerParams(
             collective_id=0, has_side_effects=True, vmem_limit_bytes=65000 * 1024
         ),
-    )(tokens, meta, *swaps, w_gate.reshape(width, hidden), w_up.reshape(width, hidden), w_down.reshape(hidden, width))
+    )(tokens, expert_ids.T, slot_positions.T, gate_probs.T, *swaps,
+      w_gate.reshape(width, hidden), w_up.reshape(width, hidden), w_down.reshape(hidden, width))
     return results[0]
 
 

time: 228 us -> 215 us (0.943)
  Pallas kernels: 223 us -> 212 us
    pallas_call x1, Pallas kernels: 223 us -> 212 us  [shards(): pl.pallas_call(functools.partial(kernel, groups, widths, starts), out_sha...]
where the time goes in v3:
time: 215 us; the launch traced here: 214 us
  Pallas kernels  212 us (99%)
  local copies, waits for them, and re-layouts  2.29 us (1%)
    pallas_call x1, Pallas kernels, shards(): pl.pallas_call(functools.partial(kernel, groups, widths, starts), out_sha...  212 us

profile of v3, /device:TPU:1, one launch (start us, length us, event | category | flops | bytes accessed | tf_op | source)
XLA Modules:
  0.0 214.4 jit_solution(8158466889243476064)
XLA Ops:
  0.0 212.1 %shard_map.91 = (bf16[128,4096]{1,0:T(8,128)(2,1)}, bf16[4,4,48,1408]{3,2,1,0:T(8,128)(2,1)}, bf16[4,4,48,1408]{3,2,1,0:T(8,128)(2,1)}, bf16[4,4,48,1280]{3,2,1,...) custom-call(bf16[128,4096]{1,0:T(8,128)(2,1)} %tok.1, ...), custom_call_target="tpu_custom_call" | custom-call | tf_op jit(solution)/shard_map/pallas_call | solution.py:605
  212.1 2.3 %copy.11 = bf16[128,4096]{1,0:T(8,128)(2,1)} copy(bf16[128,4096]{1,0:T(8,128)(2,1)} %get-tuple-element.6) | data formatting | bytes 2097152

commit v4 on v3

--- a/solution.py
+++ b/solution.py
@@ -263,7 +263,7 @@
             for r in range(3):
                 if i > 0:
                     second_send(a, r, i - 1).wait_recv()
-                for j in range(3):
+                for j in (1, 0, 2):
                     third_send(a, r, i, j).start()
                 third_local(a, r, i).start()
 
@@ -400,7 +400,7 @@
             for r in range(3):
                 if i > 0:
                     fourth_send(a, part, r, i - 1).wait_recv()
-                for j in range(3):
+                for j in (1, 0, 2):
                     fifth_send(a, part, r, i, j).start()
                 fifth_local(a, part, r, i).start()
 

time: 215 us -> 214 us (level)
  no operation moved by 1% of the time
where the time goes in v4:
time: 214 us
  Pallas kernels  212 us (99%)
  local copies, waits for them, and re-layouts  2.29 us (1%)
    pallas_call x1, Pallas kernels, shards(): pl.pallas_call(functools.partial(kernel, groups, widths, starts), out_sha...  212 us

profile of v4, /device:TPU:1, one launch (start us, length us, event | category | flops | bytes accessed | tf_op | source)
XLA Modules:
  0.0 214.0 jit_solution(9446132005082480861)
XLA Ops:
  0.0 211.7 %shard_map.91 = (bf16[128,4096]{1,0:T(8,128)(2,1)}, bf16[4,4,48,1408]{3,2,1,0:T(8,128)(2,1)}, bf16[4,4,48,1408]{3,2,1,0:T(8,128)(2,1)}, bf16[4,4,48,1280]{3,2,1,...) custom-call(bf16[128,4096]{1,0:T(8,128)(2,1)} %tok.1, ...), custom_call_target="tpu_custom_call" | custom-call | tf_op jit(solution)/shard_map/pallas_call | solution.py:605
  211.7 2.3 %copy.11 = bf16[128,4096]{1,0:T(8,128)(2,1)} copy(bf16[128,4096]{1,0:T(8,128)(2,1)} %get-tuple-element.6) | data formatting | bytes 2097152
